TPU v7x, 256 devices: a whole 4x4x8 slice. The times are simulated.
256 devices in a mesh: ctx: 32 (over z, x_lo, core), head: 8 (over x_hi, y).
Axes of the slice: x: 4 (x_hi: 2, x_lo: 2; x = x_hi * 2 + x_lo), y: 4, z: 8, core: 2. Of those that a mesh axis runs over, the one named last changes fastest.
Arguments:
- query: bfloat16 [8192, 8, 128], P('ctx', 'head'), may hold values from -8 to 8
- key: bfloat16 [8192, 128], P('ctx'), may hold values from -8 to 8
- value: bfloat16 [8192, 128], P('ctx'), may hold values from -6 to 6
- grad_out: bfloat16 [8192, 8, 128], P('ctx', 'head'), may hold values from -96 to 96
- doc_ids: int32 [8192], replicated, may hold values from 0 to 7, never falling along the last dimension, each value on 1 to 4096 neighbouring positions
- tile_mask: int32 [64, 64], replicated, may hold values from 0 to 1, as said below
Outputs:
- grad_query: bfloat16 [8192, 8, 128], P('ctx', 'head')
- grad_key: bfloat16 [8192, 128], P('ctx')
- grad_value: bfloat16 [8192, 128], P('ctx')
Inputs may be any that keep to these rules, and one draw needn't show every extreme that they name: `tile_mask`: tiles on the diagonal are 1.
All inputs are finite; a program needn't handle non-finite values.
Results may differ from a plain program's by a relative error of at most 0.011.
Values may be sent and summed in bfloat16 or wider, within the bound.
A program may use at most 64 MiB of HBM per device.

v0:
```python
import functools

import jax
import jax.numpy as jnp
from jax import lax
from jax.experimental import pallas as pl
from jax.experimental.pallas import tpu as pltpu
from jax.sharding import PartitionSpec as P

MESH = pl.DeviceIdType.MESH
BF, F32 = jnp.bfloat16, jnp.float32
SCALE = 128 ** -0.5
SCALE_2 = SCALE * 1.4426950408889634
CLOSED = -131072.0
TILES_MOD, DOC_AT, LOW_AT, HIGH_AT = 48, 48, 56, 88


def dot_nt(a, b):
    return lax.dot_general(a, b, (((1,), (1,)), ((), ())), preferred_element_type=F32)


def dot_nn(a, b):
    return lax.dot_general(a, b, (((1,), (0,)), ((), ())), preferred_element_type=F32)


def dot_tn(a, b):
    return lax.dot_general(a, b, (((0,), (0,)), ((), ())), preferred_element_type=F32)


def kernel(
    q_ref, do_ref, k_ref, v_ref, doc_ref, tm_ref,
    gq_ref, gk_ref, gv_ref,
    kv, kf, qd, qf, doc_in, tm_in, doc_t, tm_row, sc, dp, cm, cl, cd, st, st_in, acc, dq_t,
    sq, rq, sd, rd, sx, rx, sz, rz, fin, gq,
    o_s, i_s, z_s, z_r, y_s, y_r, x_s, x_r, c_s, c_r, st_s, st_r, q_s, q_r,
    d_s, d_r, xx_s, xx_r, zz_s, zz_r, h_s, h_r,
):
    ctx, head = lax.axis_index("ctx"), lax.axis_index("head")
    z, w = ctx // 4, ctx % 4
    x_lo, core = w // 2, w % 2
    x_hi, y = head // 4, head % 4
    x = 2 * x_hi + x_lo

    def device(zt, xt, yt, ct):
        return (zt * 4 + (xt % 2) * 2 + ct, (xt // 2) * 4 + yt)

    z_dev = lambda k: device((z + k) % 8, x, y, core)
    x_dev = lambda k: device(z, (x + k) % 4, y, core)
    y_dev = lambda k: device(z, x, (y + k) % 4, core)
    c_dev = device(z, x, y, 1 - core)
    h_dev = lambda k: (ctx, (head + k) % 8)

    def remote(src, dst, s, r, to):
        return pltpu.make_async_remote_copy(
            src_ref=src, dst_ref=dst, send_sem=s, recv_sem=r, device_id=to, device_id_type=MESH
        )

    barrier = pltpu.get_barrier_semaphore()
    peers = [z_dev(k) for k in range(1, 8)] + [x_dev(k) for k in range(1, 4)] + [c_dev]
    peers += [h_dev(k) for k in range(1, 8)]
    for peer in peers:
        pl.semaphore_signal(barrier, inc=1, device_id=peer, device_id_type=MESH)

    own_rows = pl.multiple_of(y * 32 + x_hi * 16, 16)

    def rows_of(xs, cs):
        return pl.ds(pl.multiple_of(((xs % 2) * 2 + cs) * 32 + (xs // 2) * 16, 16), 16)

    my_rows = rows_of(x, core)
    loads = []
    for high in (0, 1):
        theirs = pl.ds(own_rows + 128 * high, 16)
        loads.append((v_ref.at[theirs, :], kv.at[z, high, my_rows, pl.ds(0, 128)]))
        loads.append((k_ref.at[theirs, :], kv.at[z, high, my_rows, pl.ds(128, 128)]))
    for high in (0, 1):
        theirs = pl.ds(128 * high, 128)
        loads.append((do_ref.at[theirs, :], qd.at[high, y, :, pl.ds(0, 128)]))
        loads.append((q_ref.at[theirs, :], qd.at[high, y, :, pl.ds(128, 128)]))
    loads += [(doc_ref, doc_in), (tm_ref, tm_in)]
    loads = [pltpu.make_async_copy(a, b, i_s.at[n]) for n, (a, b) in enumerate(loads)]
    for load in loads:
        load.start()

    rz[...] = jnp.zeros((2, 8, 16, 256), BF)
    for load in loads[:4]:
        load.wait()
    pl.semaphore_wait(barrier, len(peers))

    def piece(k, j, cs):
        return kv.at[(z + k) % 8, :, rows_of((x + 4 - j) % 4, cs), :]

    def wanted(part, plane, reader):
        if part:
            return plane >= reader
        return (plane <= jnp.maximum(reader, 3)) | (plane >= 7 - reader)

    def z_copy(k, part):
        mine = piece(0, 0, core).at[part]
        return remote(mine, mine, z_s.at[k, part], z_r.at[k, part], z_dev(k))

    def z_take(k, part):
        theirs = piece(8 - k, 0, core).at[part]
        return remote(theirs, theirs, z_s.at[k, part], z_r.at[k, part], z_dev(k))

    def x_copy(j, k, part):
        mine = piece(k, 0, core).at[part]
        return remote(mine, mine, x_s.at[j, k, part], x_r.at[j, k, part], x_dev(j))

    def x_take(j, k, part):
        theirs = piece(k, j, core).at[part]
        return remote(theirs, theirs, x_s.at[j, k, part], x_r.at[j, k, part], x_dev(j))

    def c_copy(j, cs):
        theirs = kv.at[:, :, rows_of((x + 4 - j) % 4, cs), :]
        return remote(theirs, theirs, c_s.at[j], c_r.at[j], c_dev)

    for k in (4, 3, 5, 2, 6, 1, 7):
        for part in (0, 1):

            @pl.when(wanted(part, z, (z + k) % 8))
            def _():
                z_copy(k, part).start()

    for load in loads[4:8]:
        load.wait()
    y_copies = []
    for k in (2, 1, 3):
        mine = qd.at[:, y]
        copy = remote(mine, mine, y_s.at[k], y_r.at[k], y_dev(k))
        copy.start()
        y_copies.append(copy)

    for j in (2, 1, 3):
        for part in (0, 1):
            x_copy(j, 0, part).start()

    def clear(n, carry):
        acc[n, 0] = jnp.zeros((128, 256), F32)
        acc[n, 1] = jnp.zeros((128, 256), F32)
        return carry

    lax.fori_loop(0, 8, clear, 0)
    for load in loads[8:]:
        load.wait()

    doc_t[...] = jnp.concatenate([doc_in[...].astype(F32), jnp.zeros((64, 128), F32)], axis=0).T
    low_tile, high_tile = ctx, 63 - ctx
    lane32 = lax.broadcasted_iota(jnp.int32, (32, 128), 1)
    sub32 = lax.broadcasted_iota(jnp.int32, (32, 128), 0)
    doc_lane = (lane32 >= DOC_AT) & (lane32 < DOC_AT + 8)
    doc_of_lane = (lane32 - DOC_AT).astype(F32)

    docs_mine = doc_t[pl.ds(pl.multiple_of(y * 32, 32), 32), :]

    def key_features(t, carry):
        doc = jnp.sum(jnp.where(lane32 == t, docs_mine, 0.0), axis=1, keepdims=True)
        hit = (lane32 == t % TILES_MOD) | (doc_lane & (doc != doc_of_lane))
        low_lane = sub32 + jnp.where(t == low_tile, LOW_AT, 1000)
        high_lane = sub32 + jnp.where(t == high_tile, HIGH_AT, 1000)
        hit = hit | (lane32 == low_lane) | (lane32 == high_lane)
        high = t // 32
        at = jnp.where(high == 1, 63 - t, t)
        rows = pl.ds(pl.multiple_of((at % 4) * 32, 32), 32)
        kf[at // 4, high, rows, :] = jnp.where(hit, 1.0, 0.0).astype(BF)
        return carry

    lax.fori_loop(0, 64, key_features, 0, unroll=8)

    def query_features():
        lane = lax.broadcasted_iota(jnp.int32, (128, 128), 1)
        sub = lax.broadcasted_iota(jnp.int32, (128, 128), 0)
        for high in (0, 1):
            tile = high_tile if high else low_tile
            first = 28 - 4 * z if high else 0
            causal_at = HIGH_AT if high else LOW_AT
            doc = jnp.sum(jnp.where(lane == tile, doc_t[...], 0.0), axis=1, keepdims=True)
            tm_row[...] = jnp.zeros((8, 128), F32)
            tm_row[:, 0:64] = jnp.broadcast_to(tm_in[pl.ds(tile, 1), :].astype(F32), (8, 64))
            row = tm_row[...]
            row_far = pltpu.roll(row, 128 - TILES_MOD, 1)
            lane8 = lax.broadcasted_iota(jnp.int32, (8, 128), 1)
            near = lane8 >= first
            tile_at = jnp.where(near, lane8, lane8 + TILES_MOD)
            is_open = (jnp.where(near, row, row_far) > 0.5) & (tile_at <= tile)
            closed = jnp.where((lane8 < TILES_MOD) & jnp.logical_not(is_open), 1.0, 0.0)[0:1, :]
            hit = jnp.broadcast_to(closed, (128, 128)) > 0.5
            own_doc = doc == (lane - DOC_AT).astype(F32)
            hit = hit | ((lane >= DOC_AT) & (lane < DOC_AT + 8) & own_doc)
            later = (lane >= causal_at) & (lane < causal_at + 32) & (y * 32 + lane - causal_at > sub)
            qf[high] = jnp.where(hit | later, CLOSED, 0.0).astype(BF)

    query_features()

    for k in (1, 7, 2, 6, 3, 5, 4):
        for part in (0, 1):

            @pl.when(wanted(part, (z + 8 - k) % 8, z))
            def _():
                z_take(k, part).wait_recv()
                for j in (2, 1, 3):
                    x_copy(j, 8 - k, part).start()

    c_copy(0, core).start()
    for j in (1, 3, 2):
        for k in (0, 7, 1, 6, 2, 5, 3, 4):
            for part in (0, 1):

                @pl.when(wanted(part, (z + k) % 8, z))
                def _():
                    x_take(j, k, part).wait_recv()

        c_copy(j, core).start()

    def send_waits():
        for k in range(8):
            for part in (0, 1):
                if k:

                    @pl.when(wanted(part, z, (z + k) % 8))
                    def _():
                        z_copy(k, part).wait_send()

                @pl.when(wanted(part, (z + k) % 8, z))
                def _():
                    for j in (1, 2, 3):
                        x_copy(j, k, part).wait_send()

        for j in range(4):
            c_copy(j, core).wait_send()

    for copy in y_copies:
        copy.wait()
    for j in range(4):
        c_copy(j, 1 - core).wait_recv()

    def query_rows(high):
        return jnp.concatenate([qd[high, a, :, 128:256] for a in range(4)], axis=0)

    def out_rows(high):
        return jnp.concatenate([qd[high, a, :, 0:128] for a in range(4)], axis=0)

    def low_chunk(i):
        return i, 0, 16 + i

    def high_chunk(i):
        near = i <= z
        plane = jnp.where(near, 7 - z + i, i - 1)
        return plane, jnp.where(near, 0, 1), jnp.where(near, plane, 8 + plane)

    chunk_of = (low_chunk, high_chunk)
    counts, groups = ((z + 4) // 4, 3), (4, 3)

    for high in (1, 0):

        group = groups[high]

        def scores(i, largest):
            chunks = [chunk_of[high](i * group + g) for g in range(group)]
            queries = jnp.concatenate(
                [query_rows(high), jnp.concatenate([qf[high]] * 4, axis=0)], axis=1
            )
            keys = [
                jnp.concatenate([kv[n, part, :, 128:256], kf[n, part]], axis=1)
                for n, part, slot in chunks
            ]
            values = [kv[n, part, :, 0:128] for n, part, slot in chunks]
            s = dot_nt(jnp.concatenate(keys, axis=0), queries)
            d = dot_nt(jnp.concatenate(values, axis=0), out_rows(high))
            largest = list(largest)
            for g, (n, part, slot) in enumerate(chunks):
                rows = slice(128 * g, 128 * g + 128)
                dp[slot] = d[rows]
                for a in range(4):
                    cols = slice(128 * a, 128 * a + 128)
                    scaled = (s[rows, cols] * SCALE_2).reshape(16, 8, 128)
                    most = jnp.max(scaled, axis=0)
                    e = jnp.exp2(scaled - most[None])
                    sc[slot, :, cols] = e.reshape(128, 128)
                    cm[slot, a] = most
                    cl[slot, a] = jnp.sum(e, axis=0)
                    cd[slot, a] = jnp.sum(e * d[rows, cols].reshape(16, 8, 128), axis=0)
                    largest[a] = jnp.maximum(largest[a], most)
            return tuple(largest)

        start = (jnp.full((8, 128), -3e38, F32),) * 4
        largest = lax.fori_loop(0, counts[high], scores, start)
        largest = [jnp.max(m, axis=0, keepdims=True) for m in largest]

        def sums(i, carry):
            totals, deltas = list(carry[0:4]), list(carry[4:8])
            for g in range(group):
                slot = chunk_of[high](i * group + g)[2]
                for a in range(4):
                    weight = jnp.exp2(cm[slot, a] - largest[a])
                    totals[a] += weight * cl[slot, a]
                    deltas[a] += weight * cd[slot, a]
            return tuple(totals + deltas)

        carry = lax.fori_loop(0, counts[high], sums, (jnp.zeros((8, 128), F32),) * 8)
        for a in range(4):
            st[high, a : a + 1, :] = largest[a]
            st[high, 4 + a : 5 + a, :] = jnp.sum(carry[a], axis=0, keepdims=True)
            st[high, 8 + a : 9 + a, :] = jnp.sum(carry[4 + a], axis=0, keepdims=True)
        st[high, 12:16, :] = jnp.zeros((4, 128), F32)
        for k in (2, 1, 3):
            remote(
                st.at[high], st_in.at[k, high], st_s.at[high, k], st_r.at[high, k], y_dev(k)
            ).start()

    def row_stats(high):
        for k in (1, 3, 2):
            remote(
                st.at[high], st_in.at[k, high], st_s.at[high, k], st_r.at[high, k], y_dev(k)
            ).wait()
        parts = [st[high]] + [st_in[k, high] for k in (1, 2, 3)]
        most = functools.reduce(jnp.maximum, [p[0:4, :] for p in parts])
        weights = [jnp.exp2(p[0:4, :] - most) for p in parts]
        total = sum(wt * p[4:8, :] for wt, p in zip(weights, parts))
        delta = sum(wt * p[8:12, :] for wt, p in zip(weights, parts)) / total
        return most, 1.0 / total, delta

    def grads_of(high, most, share, delta):
        group = groups[high]

        def grads(i, carry):
            chunks = [chunk_of[high](i * group + g) for g in range(group)]
            probs, grad_s = [], []
            for n, part, slot in chunks:
                probs_row, grad_row = [], []
                for a in range(4):
                    cols = slice(128 * a, 128 * a + 128)
                    factor = jnp.exp2(cm[slot, a] - most[a : a + 1, :]) * share[a : a + 1, :]
                    p = (sc[slot, :, cols].reshape(16, 8, 128) * factor[None]).reshape(128, 128)
                    probs_row.append(p.astype(BF))
                    grad_row.append((p * (dp[slot, :, cols] - delta[a : a + 1, :])).astype(BF))
                probs.append(jnp.concatenate(probs_row, axis=1))
                grad_s.append(jnp.concatenate(grad_row, axis=1))
            probs, grad_s = jnp.concatenate(probs, axis=0), jnp.concatenate(grad_s, axis=0)
            value_part = dot_nn(probs, out_rows(high))
            key_part = dot_nn(grad_s, query_rows(high))
            for g, (n, part, slot) in enumerate(chunks):
                rows = slice(128 * g, 128 * g + 128)
                acc[n, part, :, 0:128] += value_part[rows]
                acc[n, part, :, 128:256] += key_part[rows]
            keys = jnp.concatenate([kv[n, part, :, 128:256] for n, part, slot in chunks], axis=0)
            dq_t[high] += dot_tn(keys, grad_s)
            return carry

        return grads

    def d_copy(part, half):
        return remote(
            sd.at[part, half], rd.at[part, half], d_s.at[part, half], d_r.at[part, half], c_dev
        )

    def split(part, half):
        def step(n, carry):
            for h in (0, 1):
                rows = pl.ds(pl.multiple_of((2 * h + 1 - core) * 32, 32), 32)
                sd[part, half, n, h] = acc[4 * half + n, part, rows, :].astype(BF)
            return carry

        lax.fori_loop(0, 4, step, 0, unroll=True)
        d_copy(part, half).start()

    def xx_copy(part, half, k):
        return remote(
            sx.at[part, half, (x + k) % 4], rx.at[part, half, k],
            xx_s.at[part, half, k], xx_r.at[part, half, k], x_dev(k),
        )

    def sum_cores(part, half):
        d_copy(part, half).wait()

        def step(n, carry):
            for h in (0, 1):
                rows = pl.ds(pl.multiple_of((2 * h + core) * 32, 32), 32)
                both = acc[4 * half + n, part, rows, :] + rd[part, half, n, h].astype(F32)
                both = both.astype(BF)
                sx[part, half, h, n] = both[0:16]
                sx[part, half, 2 + h, n] = both[16:32]
            return carry

        lax.fori_loop(0, 4, step, 0, unroll=True)
        for k in (2, 1, 3):
            xx_copy(part, half, k).start()

    def zz_copy(part, k):
        return remote(
            sz.at[part, (z + k) % 8], rz.at[part, k], zz_s.at[part, k], zz_r.at[part, k], z_dev(k)
        )

    def meets(part, source, target):
        return (target >= source) if part else ((target <= source) | (target >= 7 - source))

    def sum_x(part, half):
        for k in (1, 3, 2):
            xx_copy(part, half, k).wait()

        def step(n, carry):
            total = sx[part, half, x, n].astype(F32)
            total += sum(rx[part, half, k, n].astype(F32) for k in (1, 2, 3))
            sz[part, 4 * half + n] = total.astype(BF)
            return carry

        lax.fori_loop(0, 4, step, 0, unroll=True)
        for k in (4, 3, 5, 2, 6, 1, 7):
            target = (z + k) % 8

            @pl.when((target // 4 == half) & meets(part, z, target))
            def _():
                zz_copy(part, k).start()

    def h_copy(part, k):
        mine = fin.at[part, pl.ds(own_rows, 16), :]
        return remote(mine, mine, h_s.at[part, k], h_r.at[part, k], h_dev(k))

    def sum_z(part):
        for k in (1, 7, 2, 6, 3, 5, 4):

            @pl.when(meets(part, (z + 8 - k) % 8, z))
            def _():
                zz_copy(part, k).wait_recv()

        total = sz[part, z].astype(F32) + sum(rz[part, k].astype(F32) for k in range(1, 8))
        total = jnp.concatenate([total[:, 0:128], total[:, 128:256] * SCALE], axis=1)
        fin[part, pl.ds(own_rows, 16), :] = total.astype(BF)
        for k in (6, 2, 4, 1, 3, 5, 7):
            h_copy(part, k).start()

    def stores(part):
        rows = pl.ds(128 * part, 128)
        return [
            pltpu.make_async_copy(fin.at[part, :, pl.ds(0, 128)], gv_ref.at[rows, :], o_s.at[part, 0]),
            pltpu.make_async_copy(fin.at[part, :, pl.ds(128, 128)], gk_ref.at[rows, :], o_s.at[part, 1]),
        ]

    def gathered(part):
        for k in (4, 1, 7, 3, 5, 2, 6):
            sender = (head + 8 - k) % 8
            rows = pl.multiple_of((sender % 4) * 32 + (sender // 4) * 16, 16)
            theirs = fin.at[part, pl.ds(rows, 16), :]
            remote(theirs, theirs, h_s.at[part, k], h_r.at[part, k], h_dev(k)).wait_recv()
        for copy in stores(part):
            copy.start()

    dq_t[...] = jnp.zeros((2, 128, 512), F32)
    high_grads = grads_of(1, *row_stats(1))
    lax.fori_loop(0, 3, high_grads, 0)
    split(1, 1)

    @pl.when(z < 4)
    def _():
        split(1, 0)

    low_grads = grads_of(0, *row_stats(0))
    sum_cores(1, 1)
    low_grads(0, 0)
    split(0, 0)

    @pl.when(z < 4)
    def _():
        sum_cores(1, 0)

    @pl.when(z >= 4)
    def _():
        low_grads(1, 0)

    split(0, 1)

    sum_cores(0, 0)
    for a in range(4):
        for high in (0, 1):
            rows = slice(128 * high, 128 * high + 128)
            sq[a, rows, :] = dq_t[high, :, 128 * a : 128 * a + 128].T.astype(BF)
    sum_cores(0, 1)
    q_copies = []
    for k in (2, 1, 3):
        copy = remote(sq.at[(y + k) % 4], rq.at[k], q_s.at[k], q_r.at[k], y_dev(k))
        copy.start()
        q_copies.append(copy)
    sum_x(1, 1)

    @pl.when(z < 4)
    def _():
        sum_x(1, 0)

    sum_x(0, 0)
    send_waits()
    sum_x(0, 1)
    for copy in q_copies:
        copy.wait()
    total = sq[y].astype(F32) + sum(rq[k].astype(F32) for k in (1, 2, 3))
    gq[...] = (SCALE * total).astype(BF)
    gq_store = pltpu.make_async_copy(gq, gq_ref, o_s.at[2, 0])
    gq_store.start()
    sum_z(1)
    sum_z(0)
    gathered(1)
    gathered(0)
    for part in (1, 0):
        for k in range(1, 8):
            h_copy(part, k).wait_send()

            @pl.when(meets(part, z, (z + k) % 8))
            def _():
                zz_copy(part, k).wait_send()

        for copy in stores(part):
            copy.wait()
    gq_store.wait()


def write_out(a, b, c, a_out, b_out, c_out, a_mid, b_mid, c_mid, sems):
    mids = (a_mid, b_mid, c_mid)
    first = [pltpu.make_async_copy(r, m, sems.at[n, 0]) for n, (r, m) in enumerate(zip((a, b, c), mids))]
    last = [pltpu.make_async_copy(m, r, sems.at[n, 1]) for n, (r, m) in enumerate(zip((a_out, b_out, c_out), mids))]
    for copy in first:
        copy.start()
    for one, two in zip(first, last):
        one.wait()
        two.start()
    for copy in last:
        copy.wait()


def body(query, key, value, grad_out, doc_ids, tile_mask):
    hbm = pl.BlockSpec(memory_space=pltpu.HBM)
    dma = lambda *shape: pltpu.SemaphoreType.DMA(shape)
    scratch = [
        pltpu.VMEM((8, 2, 128, 256), BF),
        pltpu.VMEM((8, 2, 128, 128), BF),
        pltpu.VMEM((2, 4, 128, 256), BF),
        pltpu.VMEM((2, 128, 128), BF),
        pltpu.VMEM((64, 128), jnp.int32),
        pltpu.VMEM((64, 64), jnp.int32),
        pltpu.VMEM((128, 128), F32),
        pltpu.VMEM((8, 128), F32),
        pltpu.VMEM((24, 128, 512), F32),
        pltpu.VMEM((24, 128, 512), F32),
        pltpu.VMEM((24, 4, 8, 128), F32),
        pltpu.VMEM((24, 4, 8, 128), F32),
        pltpu.VMEM((24, 4, 8, 128), F32),
        pltpu.VMEM((2, 16, 128), F32),
        pltpu.VMEM((4, 2, 16, 128), F32),
        pltpu.VMEM((8, 2, 128, 256), F32),
        pltpu.VMEM((2, 128, 512), F32),
        pltpu.VMEM((4, 256, 128), BF),
        pltpu.VMEM((4, 256, 128), BF),
        pltpu.VMEM((2, 2, 4, 2, 32, 256), BF),
        pltpu.VMEM((2, 2, 4, 2, 32, 256), BF),
        pltpu.VMEM((2, 2, 4, 4, 16, 256), BF),
        pltpu.VMEM((2, 2, 4, 4, 16, 256), BF),
        pltpu.VMEM((2, 8, 16, 256), BF),
        pltpu.VMEM((2, 8, 16, 256), BF),
        pltpu.VMEM((2, 128, 256), BF),
        pltpu.VMEM((256, 128), BF),
        dma(3, 2),
        dma(10), dma(8, 2), dma(8, 2), dma(4), dma(4), dma(4, 8, 2), dma(4, 8, 2), dma(4), dma(4),
        dma(2, 4), dma(2, 4), dma(4), dma(4),
        dma(2, 2), dma(2, 2), dma(2, 2, 4), dma(2, 2, 4), dma(2, 8), dma(2, 8), dma(2, 8), dma(2, 8),
    ]
    grad_query, grad_key, grad_value = pl.pallas_call(
        kernel,
        out_shape=[jax.ShapeDtypeStruct((256, 128), BF)] * 3,
        in_specs=[hbm] * 6,
        out_specs=[hbm] * 3,
        scratch_shapes=scratch,
        compiler_params=pltpu.CompilerParams(
            collective_id=0, has_side_effects=True, vmem_limit_bytes=56 << 20
        ),
        cost_estimate=pl.CostEstimate(flops=3 << 30, bytes_accessed=1 << 20, transcendentals=1 << 20),
        name="attention_grads",
    )(
        query.reshape(256, 128),
        grad_out.reshape(256, 128),
        key,
        value,
        doc_ids.reshape(64, 128),
        tile_mask,
    )
    grad_query, grad_key, grad_value = pl.pallas_call(
        write_out,
        out_shape=[jax.ShapeDtypeStruct((256, 128), BF)] * 3,
        in_specs=[hbm] * 3,
        out_specs=[hbm] * 3,
        scratch_shapes=[pltpu.VMEM((256, 128), BF)] * 3 + [dma(3, 2)],
        compiler_params=pltpu.CompilerParams(vmem_limit_bytes=56 << 20),
        name="write_out",
    )(grad_query, grad_key, grad_value)
    return grad_query.reshape(256, 1, 128), grad_key, grad_value


def solution(mesh):
    rows, heads = P("ctx", None), P("ctx", "head", None)
    return jax.shard_map(
        body,
        mesh=mesh,
        in_specs=(heads, rows, rows, heads, P(), P()),
        out_specs=(heads, rows, rows),
        check_vma=False,
    )
```

profile of v0, /device:TPU:2, one launch (start us, length us, event | category | flops | bytes accessed | tf_op | source)
XLA Modules:
  0.0 47.3 jit_solution(5875180822771575073)
XLA Ops:
  0.6 45.1 %attention_grads.1 = (bf16[256,128]{1,0:T(8,128)(2,1)}, bf16[256,128]{1,0:T(8,128)(2,1)}, bf16[256,128]{1,0:T(8,128)(2,1)}) custom-call(bf16[256,128]{1,0:T(8,128)(2,1)} %bitcast.4, bf16[256,128]{1,0:T(8,128)(2,1)} %bitcast.5, bf16[256,128]{1,0:T(8,128)(2,1)} %k_ref.1, bf16[256,128]{1,0:T(8,128)(2,1)} %v_ref.1, s32[64,128]{1,0:T(8,128)} %bitcast.7, ...), custom_call_target="tpu_custom_call" | custom-call | flops 3221225472 | bytes 1048576 | tf_op jit(solution)/shard_map/attention_grads/pallas_call | solution.py:563
  45.7 1.6 %write_out.1 = (bf16[256,128]{1,0:T(8,128)(2,1)}, bf16[256,128]{1,0:T(8,128)(2,1)}, bf16[256,128]{1,0:T(8,128)(2,1)}) custom-call(bf16[256,128]{1,0:T(8,128)(2,1)} %get-tuple-element.9.a, bf16[256,128]{1,0:T(8,128)(2,1)} %get-tuple-element.10.b, bf16[256,128]{1,0:T(8,128)(2,1)} %get-tuple-element.11.c), custom_call_target="tpu_custom_call" | custom-call | tf_op jit(solution)/shard_map/write_out/pallas_call | solution.py:582
where the time goes:
time: 47.5 us; the launch traced here: 47.3 us
  Pallas kernels  46.7 us (98%)
  between operations  0.64 us (1%)
    pallas_call x1, Pallas kernels, body(): pl.pallas_call(kernel, out_shape=[jax.ShapeDtypeStruct((256, 128), BF)] *...  45.1 us
    pallas_call x1, Pallas kernels, body(): pl.pallas_call(write_out, out_shape=[jax.ShapeDtypeStruct((256, 128), BF)...  1.58 us

commit v1 on v0

--- a/solution.py
+++ b/solution.py
@@ -248,7 +248,7 @@
         return plane, jnp.where(near, 0, 1), jnp.where(near, plane, 8 + plane)
 
     chunk_of = (low_chunk, high_chunk)
-    counts, groups = ((z + 4) // 4, 3), (4, 3)
+    counts, groups = ((z + 4) // 4, 1), (4, 9)
 
     for high in (1, 0):
 
@@ -446,13 +446,19 @@
 
     dq_t[...] = jnp.zeros((2, 128, 512), F32)
     high_grads = grads_of(1, *row_stats(1))
-    lax.fori_loop(0, 3, high_grads, 0)
+    lax.fori_loop(0, 1, high_grads, 0)
     split(1, 1)
 
     @pl.when(z < 4)
     def _():
         split(1, 0)
 
+    def turn(high):
+        for a in range(4):
+            rows = slice(128 * high, 128 * high + 128)
+            sq[a, rows, :] = dq_t[high, :, 128 * a : 128 * a + 128].T.astype(BF)
+
+    turn(1)
     low_grads = grads_of(0, *row_stats(0))
     sum_cores(1, 1)
     low_grads(0, 0)
@@ -469,10 +475,7 @@
     split(0, 1)
 
     sum_cores(0, 0)
-    for a in range(4):
-        for high in (0, 1):
-            rows = slice(128 * high, 128 * high + 128)
-            sq[a, rows, :] = dq_t[high, :, 128 * a : 128 * a + 128].T.astype(BF)
+    turn(0)
     sum_cores(0, 1)
     q_copies = []
     for k in (2, 1, 3):
@@ -486,7 +489,6 @@
         sum_x(1, 0)
 
     sum_x(0, 0)
-    send_waits()
     sum_x(0, 1)
     for copy in q_copies:
         copy.wait()
@@ -494,6 +496,7 @@
     gq[...] = (SCALE * total).astype(BF)
     gq_store = pltpu.make_async_copy(gq, gq_ref, o_s.at[2, 0])
     gq_store.start()
+    send_waits()
     sum_z(1)
     sum_z(0)
     gathered(1)

time: 47.5 us -> 47 us (0.989)
  Pallas kernels: 46.7 us -> 46.2 us
    pallas_call x1, Pallas kernels: 45.1 us -> 44.6 us  [body(): pl.pallas_call(kernel, out_shape=[jax.ShapeDtypeStruct((256, 128), BF)] *...]
where the time goes in v1:
time: 47 us; the launch traced here: 46.8 us
  Pallas kernels  46.2 us (98%)
  between operations  0.64 us (1%)
    pallas_call x1, Pallas kernels, body(): pl.pallas_call(kernel, out_shape=[jax.ShapeDtypeStruct((256, 128), BF)] *...  44.6 us
    pallas_call x1, Pallas kernels, body(): pl.pallas_call(write_out, out_shape=[jax.ShapeDtypeStruct((256, 128), BF)...  1.58 us

profile of v1, /device:TPU:2, one launch (start us, length us, event | category | flops | bytes accessed | tf_op | source)
XLA Modules:
  0.0 46.8 jit_solution(11415519514216338407)
XLA Ops:
  0.6 44.6 %attention_grads.1 = (bf16[256,128]{1,0:T(8,128)(2,1)}, bf16[256,128]{1,0:T(8,128)(2,1)}, bf16[256,128]{1,0:T(8,128)(2,1)}) custom-call(bf16[256,128]{1,0:T(8,128)(2,1)} %bitcast.4, bf16[256,128]{1,0:T(8,128)(2,1)} %bitcast.5, bf16[256,128]{1,0:T(8,128)(2,1)} %k_ref.1, bf16[256,128]{1,0:T(8,128)(2,1)} %v_ref.1, s32[64,128]{1,0:T(8,128)} %bitcast.7, ...), custom_call_target="tpu_custom_call" | custom-call | flops 3221225472 | bytes 1048576 | tf_op jit(solution)/shard_map/attention_grads/pallas_call | solution.py:566
  45.2 1.6 %write_out.1 = (bf16[256,128]{1,0:T(8,128)(2,1)}, bf16[256,128]{1,0:T(8,128)(2,1)}, bf16[256,128]{1,0:T(8,128)(2,1)}) custom-call(bf16[256,128]{1,0:T(8,128)(2,1)} %get-tuple-element.9.a, bf16[256,128]{1,0:T(8,128)(2,1)} %get-tuple-element.10.b, bf16[256,128]{1,0:T(8,128)(2,1)} %get-tuple-element.11.c), custom_call_target="tpu_custom_call" | custom-call | tf_op jit(solution)/shard_map/write_out/pallas_call | solution.py:585
